TPU v7x, 32 devices: a whole 2x2x4 slice. The times are simulated.
32 devices in a mesh: ctx: 8 (over z, x), tp: 4 (over y, core).
Axes of the slice: x: 2, y: 2, z: 4, core: 2. Of those that a mesh axis runs over, the one named last changes fastest.
Arguments:
- projections: bfloat16 [2048, 3, 8192], P('ctx', None, 'tp'), may hold values from -6 to 6
- short_filter: float32 [3, 3, 8192], P(None, None, 'tp'), may hold values from -3 to 3
- decay_rates: float32 [16, 8192], P(None, 'tp'), may hold values from 1.4648437e-05 to 1
- residues: float32 [16, 8192], P(None, 'tp'), may hold values from -2.4 to 2.4
- out_weight: bfloat16 [8192, 4096], P('tp'), may hold values from -0.0625 to 0.0625
Outputs:
- projected: bfloat16 [2048, 4096], P(('ctx', 'tp'))
All inputs are finite; a program needn't handle non-finite values.
Results may differ from a plain program's by a relative error of at most 0.005.
Values may be sent and summed in bfloat16 or wider, within the bound.
A program may use at most 320 MiB of HBM per device.

v0:
```python
import functools

import jax
import jax.numpy as jnp
from jax import lax
from jax.experimental import pallas as pl
from jax.experimental.pallas import tpu as pltpu
from jax.sharding import PartitionSpec as P

LANES = 128
CHUNKS = 8
PAD = 8
GROUPS = 4
WIDTH = 512
UNROLL = 8
MESH = pl.DeviceIdType.MESH
F32 = jnp.float32
BF16 = jnp.bfloat16


def summed(terms):
    while terms.shape[0] % 2 == 0:
        middle = terms.shape[0] // 2
        terms = terms[:middle] + terms[middle:]
    return jnp.sum(terms, axis=0)


def kernel(
    n_ctx, x_hbm, taps_ref, rates_ref, res_ref, w_hbm, out_ref,
    xb, xs, pf, qf, yl, gs, ga, gb, wv, pt, excl, fades, halo_out, halo_in, st_out, twin_in, both_out, st_in,
    own_end, decay_all, carry, first, keep, kept, pair_out, pair_in, own_out, own_in, far_out, far_in,
    x_sem, w_sem, halo_sem, twin_send, twin_recv, st_send, st_recv,
    pair_send, pair_recv, own_send, own_recv, far_send, far_recv,
):
    me = lax.axis_index("ctx")
    tp = lax.axis_index("tp")
    pair, odd = me // 2, me % 2
    twin = pair * 2 + (1 - odd)
    chip, core = tp // 2, tp % 2
    sibling = chip * 2 + (1 - core)
    opposite = (1 - chip) * 2 + core
    toks, channels = xb.shape[1], xb.shape[2]
    half = toks // 2
    step = half // CHUNKS
    apart = step + 1
    tiles = channels // LANES
    per_group = tiles // GROUPS
    gwidth = channels // GROUPS
    n_out = w_hbm.shape[1] // WIDTH
    share = toks // 4
    base_a = (1 - chip) * (CHUNKS * apart)
    base_b = chip * (CHUNKS * apart)

    x_copy = pltpu.make_async_copy(x_hbm, xb, x_sem)
    x_copy.start()
    w_copy = pltpu.make_async_copy(w_hbm, wv, w_sem)

    barrier = pltpu.get_barrier_semaphore()

    @pl.loop(1, n_ctx)
    def _(k):
        pl.semaphore_signal(
            barrier, inc=1, device_id=(lax.rem(me + k, n_ctx), tp), device_id_type=MESH
        )

    for other in (sibling, opposite):
        pl.semaphore_signal(barrier, inc=1, device_id=(me, other), device_id_type=MESH)

    x_copy.wait()
    w_copy.start()
    for j in range(3):
        tail = xb[j, toks - 16 :, :].astype(F32)
        halo_out[2 * j : 2 * j + 2, :] = tail[14:16]
    halo_out[6:8, :] = jnp.zeros((2, channels), F32)

    pl.semaphore_wait(barrier, n_ctx + 1)

    halo_copy = pltpu.make_async_remote_copy(
        src_ref=halo_out, dst_ref=halo_in, send_sem=halo_sem.at[0], recv_sem=halo_sem.at[1],
        device_id=(lax.rem(me + 1, n_ctx), tp), device_id_type=MESH,
    )

    @pl.when(me < n_ctx - 1)
    def _():
        halo_copy.start()

    def features(c, lane, rows):
        feats = []
        for j in range(3):
            total = taps_ref[0, j : j + 1, lane] * xs[j, c, PAD : PAD + rows, :]
            for i in (1, 2):
                total += taps_ref[i, j : j + 1, lane] * xs[j, c, PAD - i : PAD - i + rows, :]
            feats.append(total)
        product = feats[1] * feats[2]
        for low in range(0, rows, step):
            high = min(low + step, rows)
            at = low // step * apart
            qf[c, at : at + high - low, :] = feats[0][low:high]
            pf[c, at : at + high - low, :] = product[low:high]

    @pl.loop(0, tiles)
    def _(c):
        lane = pl.ds(pl.multiple_of(c * LANES, LANES), LANES)
        for j in range(3):
            xs[j, c, :PAD, :] = jnp.zeros((PAD, LANES), F32)
            xs[j, c, PAD:, :] = xb[j, :, lane].astype(F32)
        features(c, lane, toks)

    @pl.when(me == 0)
    def _():
        halo_in[...] = jnp.zeros_like(halo_in)

    @pl.when(me > 0)
    def _():
        halo_copy.wait_recv()

    place = lax.broadcasted_iota(jnp.int32, (1, CHUNKS, LANES), 1)

    def spread(rows):
        return jnp.broadcast_to(rows[:, None, :], (rows.shape[0], CHUNKS, LANES))

    def scanned(state, rates):
        for reach in (1, 2, 4):
            fade = spread(jnp.exp(-rates * float(step * reach)))
            moved = pltpu.roll(state, reach, 1)
            state = state + jnp.where(place >= reach, fade * moved, 0.0)
        return jnp.where(place >= 1, pltpu.roll(state, 1, 1), 0.0), state[:, CHUNKS - 1, :]

    def local_tile(c):
        lane = pl.ds(pl.multiple_of(c * LANES, LANES), LANES)
        rates = rates_ref[:, lane]
        decay = spread(jnp.exp(-rates))
        weight = spread(res_ref[:, lane] * jnp.sqrt(2.0 * rates))
        for j in range(3):
            xs[j, c, PAD - 2 : PAD, :] = halo_in[2 * j : 2 * j + 2, lane]
        features(c, lane, 8)
        zero = jnp.zeros((rates.shape[0], CHUNKS, LANES), F32)

        def ends(outer, state):
            for k in range(UNROLL):
                rows = pl.ds(base_b + outer * UNROLL + k, CHUNKS, stride=apart)
                state = decay * state + pf[c, rows, :][None]
            return state

        before_b, total_b = scanned(lax.fori_loop(0, step // UNROLL, ends, zero), rates)
        excl[1, c] = before_b

        def both(outer, state):
            for k in range(UNROLL):
                rows = pl.ds(base_a + outer * UNROLL + k, CHUNKS, stride=apart)
                state = decay * state + pf[c, rows, :][None]
                yl[c, pl.ds(outer * UNROLL + k, CHUNKS, stride=apart), :] = summed(weight * state)
            return state

        before_a, total_a = scanned(lax.fori_loop(0, step // UNROLL, both, zero), rates)
        excl[0, c] = before_a
        fade = jnp.exp(-rates * float(half))
        early = jnp.where(chip == 0, total_b, total_a)
        late = jnp.where(chip == 0, total_a, total_b)
        first[:, lane] = early
        end = fade * early + late
        own_end[:, lane] = end
        st_out[:, lane] = end.astype(BF16)
        decay_all[:, lane] = jnp.exp(-rates * float(toks))

    def group(g):
        return pl.ds(g * gwidth, gwidth)

    def twin_copy(g):
        return pltpu.make_async_remote_copy(
            src_ref=st_out.at[:, group(g)], dst_ref=twin_in.at[:, group(g)],
            send_sem=twin_send.at[g], recv_sem=twin_recv.at[g],
            device_id=(twin, tp), device_id_type=MESH,
        )

    def state_copy(g, src, dst):
        return pltpu.make_async_remote_copy(
            src_ref=both_out.at[:, group(g)], dst_ref=st_in.at[src, :, group(g)],
            send_sem=st_send.at[dst, g], recv_sem=st_recv.at[src, g],
            device_id=(dst * 2 + odd, tp), device_id_type=MESH,
        )

    def send_both(g):
        cols = group(g)
        twin_copy(g).wait_recv()
        other = twin_in[:, cols].astype(F32)
        own = own_end[:, cols]
        fade = decay_all[:, cols]
        total = jnp.where(odd == 1, fade * other + own, fade * own + other)
        both_out[:, cols] = total.astype(BF16)

        @pl.loop(pair + 1, n_ctx // 2)
        def _(dst):
            state_copy(g, pair, dst).start()

    for g in range(GROUPS):
        @pl.loop(g * per_group, (g + 1) * per_group)
        def _(c):
            local_tile(c)

        twin_copy(g).start()
        if g > 0:
            send_both(g - 1)
    send_both(GROUPS - 1)

    def steady(c):
        lane = pl.ds(pl.multiple_of(c * LANES, LANES), LANES)
        rates = rates_ref[:, lane]
        weight = spread(res_ref[:, lane] * jnp.sqrt(2.0 * rates) * jnp.exp(-rates))
        starts = (place * step).astype(F32)
        fade = weight * jnp.exp(-spread(rates) * starts)
        base = weight * excl[0, c]
        fades[c] = fade
        excl[0, c] = base + jnp.where(chip == 0, fade * spread(first[:, lane]), 0.0)

    @pl.loop(0, tiles)
    def _(c):
        steady(c)

    def entering(c, lane, rates):
        starts = (place * step).astype(F32)
        into = carry[:, lane]
        late = jnp.exp(-rates * float(half)) * into + first[:, lane]
        into = jnp.where(chip == 1, late, into)
        return excl[1, c] + jnp.exp(-spread(rates) * starts) * spread(into)

    def carried_tile(c):
        lane = pl.ds(pl.multiple_of(c * LANES, LANES), LANES)
        rates = rates_ref[:, lane]
        decay = spread(jnp.exp(-rates))
        into = carry[:, lane]
        into = jnp.where(chip == 0, jnp.exp(-rates * float(half)) * into, into)
        state = excl[0, c] + fades[c] * spread(into)

        def some(outer, state):
            for k in range(UNROLL):
                i = outer * UNROLL + k
                local = pl.ds(i, CHUNKS, stride=apart)
                gate = qf[c, pl.ds(base_a + i, CHUNKS, stride=apart), :]
                gs[local, :] = gate * (yl[c, local, :] + summed(state))
                state = decay * state
            return state

        lax.fori_loop(0, step // UNROLL, some, state)
        for s in range(CHUNKS):
            ga[s * step : (s + 1) * step, lane] = gs[s * apart : s * apart + step, :].astype(BF16)

    def own_tile(c):
        lane = pl.ds(pl.multiple_of(c * LANES, LANES), LANES)
        rates = rates_ref[:, lane]
        decay = spread(jnp.exp(-rates))
        weight = spread(res_ref[:, lane] * jnp.sqrt(2.0 * rates))
        state = entering(c, lane, rates)

        def some(outer, state):
            for k in range(UNROLL):
                i = outer * UNROLL + k
                rows = pl.ds(base_b + i, CHUNKS, stride=apart)
                state = decay * state + pf[c, rows, :][None]
                gs[pl.ds(i, CHUNKS, stride=apart), :] = qf[c, rows, :] * summed(weight * state)
            return state

        lax.fori_loop(0, step // UNROLL, some, state)
        for s in range(CHUNKS):
            gb[s * step : (s + 1) * step, lane] = gs[s * apart : s * apart + step, :].astype(BF16)

    for g in range(GROUPS):
        cols = group(g)
        carry[:, cols] = jnp.zeros((carry.shape[0], gwidth), F32)

        @pl.loop(0, pair)
        def _(src):
            fade = decay_all[:, cols] * decay_all[:, cols]
            state_copy(g, src, pair).wait_recv()
            carry[:, cols] = fade * carry[:, cols] + st_in[src, :, cols].astype(F32)

        @pl.when(odd == 1)
        def _():
            carry[:, cols] = decay_all[:, cols] * carry[:, cols] + twin_in[:, cols].astype(F32)

        @pl.loop(g * per_group, (g + 1) * per_group)
        def _(c):
            carried_tile(c)

    w_copy.wait()

    def to_sibling(n, out, into, send, recv):
        return pltpu.make_async_remote_copy(
            src_ref=out.at[n], dst_ref=into.at[n], send_sem=send.at[n], recv_sem=recv.at[n],
            device_id=(me, sibling), device_id_type=MESH,
        )

    def pair_copy(n):
        return to_sibling(n, pair_out, pair_in, pair_send, pair_recv)

    def own_copy(n):
        return to_sibling(n, own_out, own_in, own_send, own_recv)

    def far_copy(n):
        return pltpu.make_async_remote_copy(
            src_ref=far_out.at[n], dst_ref=far_in.at[n],
            send_sem=far_send.at[n], recv_sem=far_recv.at[n],
            device_id=(me, opposite), device_id_type=MESH,
        )

    mine = pl.ds(pl.multiple_of(core * share, share), share)
    theirs = pl.ds(pl.multiple_of((1 - core) * share, share), share)

    def forward(n):
        pair_copy(n).wait_recv()
        far_out[n] = (keep[n] + pair_in[n].astype(F32)).astype(BF16)
        far_copy(n).start()

    def columns(n):
        return pl.ds(pl.multiple_of(n * WIDTH, WIDTH), WIDTH)

    @pl.loop(0, n_out)
    def _(n):
        pt[...] = jnp.dot(ga[...], wv[:, columns(n)], preferred_element_type=F32)
        pair_out[n] = pt[theirs, :].astype(BF16)
        pair_copy(n).start()
        keep[n] = pt[mine, :]

        @pl.when(n > 0)
        def _():
            forward(n - 1)

    forward(n_out - 1)

    @pl.loop(0, tiles)
    def _(c):
        own_tile(c)

    @pl.loop(0, n_out)
    def _(n):
        pt[...] = jnp.dot(gb[...], wv[:, columns(n)], preferred_element_type=F32)
        own_out[n] = pt[theirs, :].astype(BF16)
        own_copy(n).start()
        kept[n] = pt[mine, :]

    @pl.loop(0, n_out)
    def _(n):
        own_copy(n).wait_recv()
        far_copy(n).wait_recv()
        total = kept[n] + own_in[n].astype(F32) + far_in[n].astype(F32)
        out_ref[:, columns(n)] = total.astype(BF16)

    @pl.loop(0, n_out)
    def _(n):
        pair_copy(n).wait_send()
        own_copy(n).wait_send()
        far_copy(n).wait_send()

    for g in range(GROUPS):
        twin_copy(g).wait_send()

        @pl.loop(pair + 1, n_ctx // 2)
        def _(dst):
            state_copy(g, pair, dst).wait_send()

    @pl.when(me < n_ctx - 1)
    def _():
        halo_copy.wait_send()


def per_device(n_ctx, projections, short_filter, decay_rates, residues, out_weight):
    x = jnp.transpose(projections, (1, 0, 2))
    _, toks, channels = x.shape
    modes = decay_rates.shape[0]
    dout = out_weight.shape[1]
    tiles = channels // LANES
    n_out = dout // WIDTH
    share = toks // 4
    padded = toks // 2 + CHUNKS
    dma = pltpu.SemaphoreType.DMA
    vmem = pl.BlockSpec(memory_space=pltpu.VMEM)
    hbm = pl.BlockSpec(memory_space=pl.ANY)
    return pl.pallas_call(
        functools.partial(kernel, n_ctx),
        out_shape=jax.ShapeDtypeStruct((share, dout), BF16),
        in_specs=[hbm, vmem, vmem, vmem, hbm],
        out_specs=vmem,
        scratch_shapes=[
            pltpu.VMEM((3, toks, channels), BF16),
            pltpu.VMEM((3, tiles, PAD + toks, LANES), F32),
            pltpu.VMEM((tiles, 2 * padded, LANES), F32),
            pltpu.VMEM((tiles, 2 * padded, LANES), F32),
            pltpu.VMEM((tiles, padded, LANES), F32),
            pltpu.VMEM((padded, LANES), F32),
            pltpu.VMEM((toks // 2, channels), BF16),
            pltpu.VMEM((toks // 2, channels), BF16),
            pltpu.VMEM((channels, dout), BF16),
            pltpu.VMEM((toks // 2, WIDTH), F32),
            pltpu.VMEM((2, tiles, modes, CHUNKS, LANES), F32),
            pltpu.VMEM((tiles, modes, CHUNKS, LANES), F32),
            pltpu.VMEM((8, channels), F32),
            pltpu.VMEM((8, channels), F32),
            pltpu.VMEM((modes, channels), BF16),
            pltpu.VMEM((modes, channels), BF16),
            pltpu.VMEM((modes, channels), BF16),
            pltpu.VMEM((n_ctx // 2, modes, channels), BF16),
            pltpu.VMEM((modes, channels), F32),
            pltpu.VMEM((modes, channels), F32),
            pltpu.VMEM((modes, channels), F32),
            pltpu.VMEM((modes, channels), F32),
            pltpu.VMEM((n_out, share, WIDTH), F32),
            pltpu.VMEM((n_out, share, WIDTH), F32),
            pltpu.VMEM((n_out, share, WIDTH), BF16),
            pltpu.VMEM((n_out, share, WIDTH), BF16),
            pltpu.VMEM((n_out, share, WIDTH), BF16),
            pltpu.VMEM((n_out, share, WIDTH), BF16),
            pltpu.VMEM((n_out, share, WIDTH), BF16),
            pltpu.VMEM((n_out, share, WIDTH), BF16),
            dma, dma, dma((2,)),
            dma((GROUPS,)), dma((GROUPS,)),
            dma((n_ctx // 2, GROUPS)), dma((n_ctx // 2, GROUPS)),
            dma((n_out,)), dma((n_out,)), dma((n_out,)), dma((n_out,)),
            dma((n_out,)), dma((n_out,)),
        ],
        compiler_params=pltpu.CompilerParams(
            collective_id=0, has_side_effects=True, vmem_limit_bytes=58 * 2**20
        ),
    )(x, short_filter, decay_rates, residues, out_weight)


def solution(mesh):
    placed = (
        P("ctx", None, "tp"),
        P(None, None, "tp"),
        P(None, "tp"),
        P(None, "tp"),
        P("tp", None),
    )
    return jax.shard_map(
        functools.partial(per_device, mesh.shape["ctx"]),
        mesh=mesh, in_specs=placed, out_specs=P(("ctx", "tp"), None), check_vma=False,
    )
```

profile of v0, /device:TPU:0, one launch (start us, length us, event | category | flops | bytes accessed | tf_op | source)
XLA Modules:
  0.0 41.2 jit_solution(15053884316561040986)
XLA Ops:
  0.0 39.3 %shard_map.55 = bf16[64,4096]{1,0:T(8,128)(2,1)} custom-call(bf16[3,256,2048]{2,1,0:T(8,128)(2,1)} %bitcast.1, f32[3,3,2048]{2,1,0:T(4,128)} %taps_ref.1, f32[16,2048]{1,0:T(8,128)} %rates_ref.1, f32[16,2048]{1,0:T(8,128)} %res_ref.1, bf16[2048,4096]{1,0:T(8,128)(2,1)} %w_hbm.1), custom_call_target="tpu_custom_call" | custom-call | tf_op jit(solution)/shard_map/pallas_call | solution.py:378
  39.3 1.9 %copy.7 = bf16[64,4096]{1,0:T(8,128)(2,1)} copy(bf16[64,4096]{1,0:T(8,128)(2,1)} %shard_map.55) | data formatting | bytes 1048576
where the time goes:
time: 41.4 us; the launch traced here: 41.2 us
  Pallas kernels  39.3 us (95%)
  local copies, waits for them, and re-layouts  1.87 us (5%)
    pallas_call x1, Pallas kernels, per_device(): pl.pallas_call(functools.partial(kernel, n_ctx), out_shape=jax.ShapeDtype...  39.3 us
    unnamed x1, local copies, waits for them, and re-layouts  1.87 us

commit v1 on v0

v1 whole, which is shorter than its diff:
```python
import functools

import jax
import jax.numpy as jnp
from jax import lax
from jax.experimental import pallas as pl
from jax.experimental.pallas import tpu as pltpu
from jax.sharding import PartitionSpec as P

LANES = 128
CHUNKS = 8
GROUPS = 4
HALO_GROUP = 2
MXU = 256
WIDTH = 512
TAIL = 16
MESH = pl.DeviceIdType.MESH
F32 = jnp.float32
BF16 = jnp.bfloat16


def summed(terms):
    while terms.shape[0] % 2 == 0:
        middle = terms.shape[0] // 2
        terms = terms[:middle] + terms[middle:]
    return jnp.sum(terms, axis=0)


def kernel(
    n_ctx, x_hbm, taps_hbm, rates_hbm, res_hbm, w_hbm, out_ref,
    xb, tails, taps_ref, rates_ref, res_ref, order, back, xs, pf, qf, yl, gp, ga, gb, wv, pt, raw, base, fades, hb,
    halo_out, halo_in, st_out, twin_in, both_out, st_in,
    own_end, decay_all, carry, first, keep, kept, pair_out, pair_in, own_out, own_in, far_out, far_in,
    x_sem, in_sem, w_sem, halo_sem, twin_send, twin_recv, st_send, st_recv,
    pair_send, pair_recv, own_send, own_recv, far_send, far_recv,
):
    me = lax.axis_index("ctx")
    tp = lax.axis_index("tp")
    pair, odd = me // 2, me % 2
    twin = pair * 2 + (1 - odd)
    chip, core = tp // 2, tp % 2
    sibling = chip * 2 + (1 - core)
    opposite = (1 - chip) * 2 + core
    toks, channels = xb.shape[1], xb.shape[2]
    modes = rates_ref.shape[0]
    half = toks // 2
    step = half // CHUNKS
    rows = half + 2 * CHUNKS
    tiles = channels // LANES
    per_group = tiles // GROUPS
    gwidth = channels // GROUPS
    blocks = gwidth // MXU
    per_block = MXU // LANES
    n_out = w_hbm.shape[1] // WIDTH
    share = toks // 4
    early = 1 - chip

    def group(g):
        return pl.ds(g * gwidth, gwidth)

    def x_copy(g):
        return pltpu.make_async_copy(
            x_hbm.at[1:3, :, group(g)], xb.at[1:3, :, group(g)], x_sem.at[g]
        )

    tail_copy = pltpu.make_async_copy(x_hbm.at[:, toks - TAIL :, :], tails, in_sem.at[0])
    rates_copy = pltpu.make_async_copy(rates_hbm, rates_ref, in_sem.at[1])
    taps_copy = pltpu.make_async_copy(taps_hbm, taps_ref, in_sem.at[2])
    res_copy = pltpu.make_async_copy(res_hbm, res_ref, in_sem.at[3])
    gate_copy = pltpu.make_async_copy(x_hbm.at[0], xb.at[0], in_sem.at[4])
    w_copy = pltpu.make_async_copy(w_hbm, wv, w_sem)

    rates_copy.start()
    taps_copy.start()
    x_copy(0).start()
    res_copy.start()
    tail_copy.start()
    for g in range(1, GROUPS):
        x_copy(g).start()
    gate_copy.start()
    w_copy.start()

    barrier = pltpu.get_barrier_semaphore()

    @pl.loop(1, n_ctx)
    def _(k):
        pl.semaphore_signal(
            barrier, inc=1, device_id=(lax.rem(me + k, n_ctx), tp), device_id_type=MESH
        )

    for other in (sibling, opposite):
        pl.semaphore_signal(barrier, inc=1, device_id=(me, other), device_id_type=MESH)

    for b in range(2):
        row = lax.broadcasted_iota(jnp.int32, (rows, toks), 0)
        token = lax.broadcasted_iota(jnp.int32, (rows, toks), 1)
        start = early * half if b == 0 else chip * half
        wanted = start + (row % CHUNKS) * step + row // CHUNKS - 2
        order[b * rows : (b + 1) * rows, :] = jnp.where(token == wanted, 1.0, 0.0).astype(BF16)
    token = lax.broadcasted_iota(jnp.int32, (half, half), 0)
    row = lax.broadcasted_iota(jnp.int32, (half, half), 1)
    back[...] = jnp.where(token == (row % CHUNKS) * step + row // CHUNKS, 1.0, 0.0).astype(BF16)

    place = lax.broadcasted_iota(jnp.int32, (1, CHUNKS, LANES), 1)
    spots = place.astype(F32) * float(step)
    to_end = float((CHUNKS - 1) * step) - spots
    late_block = jnp.where(chip == 0, 1.0, 0.0).astype(F32)

    def spread(values):
        return jnp.broadcast_to(values[:, None, :], (values.shape[0], CHUNKS, LANES))

    def lanes(c):
        return pl.ds(pl.multiple_of(c * LANES, LANES), LANES)

    def reorder(j, k):
        cols = pl.ds(pl.multiple_of(k * MXU, MXU), MXU)
        moved = jnp.dot(order[...], xb[j, :, cols], preferred_element_type=F32)
        for b in range(2):
            for t in range(per_block):
                xs[j, b, k * per_block + t] = moved[b * rows : (b + 1) * rows, t * LANES : (t + 1) * LANES]

    def feature(j, b, c, low, high):
        lane = lanes(c)
        total = None
        for i in range(3):
            at = (2 - i) * CHUNKS
            term = taps_ref[i, j : j + 1, lane] * xs[j, b, c, at + low : at + high, :]
            total = term if total is None else total + term
        return total

    def ends(c):
        decay = spread(jnp.exp(-rates_ref[:, lanes(c)]))
        for b in range(2):
            product = feature(1, b, c, 0, half) * feature(2, b, c, 0, half)
            pf[b, c] = product
            state = jnp.broadcast_to(product[None, :CHUNKS], (modes, CHUNKS, LANES))
            for i in range(1, step):
                state = decay * state + product[None, i * CHUNKS : (i + 1) * CHUNKS]
            raw[b, c] = state

    def finish(c):
        lane = lanes(c)
        rates = rates_ref[:, lane]
        decay = spread(jnp.exp(-rates))
        two = 2 * CHUNKS
        for j in (1, 2):
            xs[j, early, c, 0:1, :] = halo_in[2 * j : 2 * j + 1, lane]
            xs[j, early, c, CHUNKS : CHUNKS + 1, :] = halo_in[2 * j + 1 : 2 * j + 2, lane]
        product = feature(1, early, c, 0, two) * feature(2, early, c, 0, two)
        change = product - pf[early, c, :two, :]
        pf[early, c, :two, :] = product
        grown = decay * change[None, :CHUNKS] + change[None, CHUNKS:]
        raw[early, c] = raw[early, c] + spread(jnp.exp(-rates * float(step - 2))) * grown
        whole = jnp.exp(-rates * float(half))
        mixed = spread(whole) * raw[early, c] + raw[chip, c]
        end = jnp.sum(jnp.exp(-spread(rates) * to_end) * mixed, axis=1)
        own_end[:, lane] = end
        st_out[:, lane] = end.astype(BF16)
        decay_all[:, lane] = jnp.exp(-rates * float(toks))

    def scanned(state, rates):
        for reach in (1, 2, 4):
            fade = spread(jnp.exp(-rates * float(step * reach)))
            moved = pltpu.roll(state, reach, 1)
            state = state + jnp.where(place >= reach, fade * moved, 0.0)
        return jnp.where(place >= 1, pltpu.roll(state, 1, 1), 0.0), state[:, CHUNKS - 1, :]

    def near(b, c):
        for i in range(step):
            total = None
            for k in range(i + 1):
                at = (i - k) * CHUNKS
                term = hb[c, k] * pf[b, c, at : at + CHUNKS, :]
                total = term if total is None else total + term
            yl[c, i * CHUNKS : (i + 1) * CHUNKS, :] = total

    def responses(c):
        lane = lanes(c)
        rates = rates_ref[:, lane]
        decay = jnp.exp(-rates)
        now = res_ref[:, lane] * jnp.sqrt(2.0 * rates)
        for i in range(step):
            hb[c, i] = jnp.broadcast_to(jnp.sum(now, axis=0, keepdims=True), (CHUNKS, LANES))
            now = now * decay

    def gates(b, c):
        lane = lanes(c)
        if b == 0:
            xs[0, early, c, 0:1, :] = halo_in[0:1, lane]
            xs[0, early, c, CHUNKS : CHUNKS + 1, :] = halo_in[1:2, lane]
        qf[c] = feature(0, b, c, 0, half)

    def weights(lane, rates):
        return res_ref[:, lane] * jnp.sqrt(2.0 * rates) * jnp.exp(-rates)

    def ahead(c):
        lane = lanes(c)
        rates = rates_ref[:, lane]
        before, total = scanned(raw[0, c], rates)
        other = jnp.sum(jnp.exp(-spread(rates) * to_end) * raw[1, c], axis=1)
        first[:, lane] = jnp.where(chip == 0, other, total)
        weight = spread(weights(lane, rates))
        into = jnp.exp(-spread(rates) * spots)
        fades[c] = weight * into * spread(jnp.exp(-rates * (float(half) * late_block)))
        base[c] = weight * (before + into * spread(other * late_block))
        gates(0, c)
        near(0, c)

    def emit(c, state):
        lane = lanes(c)
        decay = spread(jnp.exp(-rates_ref[:, lane]))
        for i in range(0, step, 2):
            parts = []
            for k in (i, i + 1):
                at = slice(k * CHUNKS, (k + 1) * CHUNKS)
                parts.append(qf[c, at, :] * (yl[c, at, :] + summed(state)))
                state = decay * state
            gp[i * CHUNKS : (i + 2) * CHUNKS, lane] = jnp.concatenate(parts, axis=0).astype(BF16)

    def carried_tile(c):
        emit(c, base[c] + fades[c] * spread(carry[:, lanes(c)]))

    def own_tile(c):
        lane = lanes(c)
        rates = rates_ref[:, lane]
        before, _ = scanned(raw[1, c], rates)
        into = carry[:, lane]
        into = jnp.where(chip == 1, jnp.exp(-rates * float(half)) * into + first[:, lane], into)
        state = spread(weights(lane, rates)) * (before + jnp.exp(-spread(rates) * spots) * spread(into))
        gates(1, c)
        near(1, c)
        emit(c, state)

    def restore(into, k):
        cols = pl.ds(pl.multiple_of(k * MXU, MXU), MXU)
        into[:, cols] = jnp.dot(back[...], gp[:, cols], preferred_element_type=F32).astype(BF16)

    halo_copy = pltpu.make_async_remote_copy(
        src_ref=halo_out, dst_ref=halo_in, send_sem=halo_sem.at[0], recv_sem=halo_sem.at[1],
        device_id=(lax.rem(me + 1, n_ctx), tp), device_id_type=MESH,
    )

    def twin_copy(g):
        return pltpu.make_async_remote_copy(
            src_ref=st_out.at[:, group(g)], dst_ref=twin_in.at[:, group(g)],
            send_sem=twin_send.at[g], recv_sem=twin_recv.at[g],
            device_id=(twin, tp), device_id_type=MESH,
        )

    def state_copy(g, src, dst):
        return pltpu.make_async_remote_copy(
            src_ref=both_out.at[:, group(g)], dst_ref=st_in.at[src, :, group(g)],
            send_sem=st_send.at[dst, g], recv_sem=st_recv.at[src, g],
            device_id=(dst * 2 + odd, tp), device_id_type=MESH,
        )

    def send_both(g):
        cols = group(g)
        twin_copy(g).wait_recv()
        other = twin_in[:, cols].astype(F32)
        own = own_end[:, cols]
        fade = decay_all[:, cols]
        total = jnp.where(odd == 1, fade * other + own, fade * own + other)
        both_out[:, cols] = total.astype(BF16)

        @pl.loop(pair + 1, n_ctx // 2)
        def _(dst):
            state_copy(g, pair, dst).start()

    def group_ends(g):
        x_copy(g).wait()

        @pl.loop(g * blocks, (g + 1) * blocks)
        def _(k):
            for j in (1, 2):
                reorder(j, k)

            @pl.loop(k * per_block, (k + 1) * per_block)
            def _(c):
                ends(c)

    def group_finish(g):
        @pl.loop(g * per_group, (g + 1) * per_group)
        def _(c):
            finish(c)

        twin_copy(g).start()

    tail_copy.wait()
    for j in range(3):
        halo_out[2 * j : 2 * j + 2, :] = tails[j].astype(F32)[TAIL - 2 :]
    halo_out[6:8, :] = jnp.zeros((2, channels), F32)
    rates_copy.wait()
    taps_copy.wait()
    group_ends(0)

    pl.semaphore_wait(barrier, n_ctx + 1)

    @pl.when(me < n_ctx - 1)
    def _():
        halo_copy.start()

    for g in range(1, GROUPS):
        group_ends(g)
        if g == HALO_GROUP:
            @pl.when(me == 0)
            def _():
                halo_in[...] = jnp.zeros_like(halo_in)

            @pl.when(me > 0)
            def _():
                halo_copy.wait_recv()

            for before in range(g):
                group_finish(before)
        if g >= HALO_GROUP:
            group_finish(g)

    res_copy.wait()
    gate_copy.wait()

    for g in range(GROUPS):
        @pl.loop(g * blocks, (g + 1) * blocks)
        def _(k):
            reorder(0, k)

            @pl.loop(k * per_block, (k + 1) * per_block)
            def _(c):
                responses(c)
                ahead(c)

        if g == GROUPS - 2:
            for sent in range(g + 1):
                send_both(sent)
    send_both(GROUPS - 1)

    for g in range(GROUPS):
        cols = group(g)
        carry[:, cols] = jnp.zeros((modes, gwidth), F32)

        @pl.loop(0, pair)
        def _(src):
            fade = decay_all[:, cols] * decay_all[:, cols]
            state_copy(g, src, pair).wait_recv()
            carry[:, cols] = fade * carry[:, cols] + st_in[src, :, cols].astype(F32)

        @pl.when(odd == 1)
        def _():
            carry[:, cols] = decay_all[:, cols] * carry[:, cols] + twin_in[:, cols].astype(F32)

        @pl.loop(g * blocks, (g + 1) * blocks)
        def _(k):
            @pl.loop(k * per_block, (k + 1) * per_block)
            def _(c):
                carried_tile(c)

            restore(ga, k)

    w_copy.wait()

    def to_sibling(n, out, into, send, recv):
        return pltpu.make_async_remote_copy(
            src_ref=out.at[n], dst_ref=into.at[n], send_sem=send.at[n], recv_sem=recv.at[n],
            device_id=(me, sibling), device_id_type=MESH,
        )

    def pair_copy(n):
        return to_sibling(n, pair_out, pair_in, pair_send, pair_recv)

    def own_copy(n):
        return to_sibling(n, own_out, own_in, own_send, own_recv)

    def far_copy(n):
        return pltpu.make_async_remote_copy(
            src_ref=far_out.at[n], dst_ref=far_in.at[n],
            send_sem=far_send.at[n], recv_sem=far_recv.at[n],
            device_id=(me, opposite), device_id_type=MESH,
        )

    mine = pl.ds(pl.multiple_of(core * share, share), share)
    theirs = pl.ds(pl.multiple_of((1 - core) * share, share), share)

    def forward(n):
        pair_copy(n).wait_recv()
        far_out[n] = (keep[n] + pair_in[n].astype(F32)).astype(BF16)
        far_copy(n).start()

    def columns(n):
        return pl.ds(pl.multiple_of(n * WIDTH, WIDTH), WIDTH)

    @pl.loop(0, n_out)
    def _(n):
        pt[...] = jnp.dot(ga[...], wv[:, columns(n)], preferred_element_type=F32)
        pair_out[n] = pt[theirs, :].astype(BF16)
        pair_copy(n).start()
        keep[n] = pt[mine, :]

        @pl.when(n > 0)
        def _():
            forward(n - 1)

    forward(n_out - 1)

    @pl.loop(0, channels // MXU)
    def _(k):
        @pl.loop(k * per_block, (k + 1) * per_block)
        def _(c):
            own_tile(c)

        restore(gb, k)

    @pl.loop(0, n_out)
    def _(n):
        pt[...] = jnp.dot(gb[...], wv[:, columns(n)], preferred_element_type=F32)
        own_out[n] = pt[theirs, :].astype(BF16)
        own_copy(n).start()
        kept[n] = pt[mine, :]

    @pl.loop(0, n_out)
    def _(n):
        own_copy(n).wait_recv()
        far_copy(n).wait_recv()
        total = kept[n] + own_in[n].astype(F32) + far_in[n].astype(F32)
        out_ref[:, columns(n)] = total.astype(BF16)

    @pl.loop(0, n_out)
    def _(n):
        pair_copy(n).wait_send()
        own_copy(n).wait_send()
        far_copy(n).wait_send()

    for g in range(GROUPS):
        twin_copy(g).wait_send()

        @pl.loop(pair + 1, n_ctx // 2)
        def _(dst):
            state_copy(g, pair, dst).wait_send()

    @pl.when(me < n_ctx - 1)
    def _():
        halo_copy.wait_send()


def per_device(n_ctx, projections, short_filter, decay_rates, residues, out_weight):
    x = jnp.transpose(projections, (1, 0, 2))
    _, toks, channels = x.shape
    modes = decay_rates.shape[0]
    dout = out_weight.shape[1]
    tiles = channels // LANES
    n_out = dout // WIDTH
    share = toks // 4
    half = toks // 2
    step = half // CHUNKS
    rows = half + 2 * CHUNKS
    dma = pltpu.SemaphoreType.DMA
    hbm = pl.BlockSpec(memory_space=pltpu.HBM)
    operands = [
        pltpu.with_memory_space_constraint(a, pltpu.HBM)
        for a in (x, short_filter, decay_rates, residues, out_weight)
    ]
    return pl.pallas_call(
        functools.partial(kernel, n_ctx),
        out_shape=jax.ShapeDtypeStruct((share, dout), BF16),
        in_specs=[hbm] * 5,
        out_specs=pl.BlockSpec(memory_space=pltpu.VMEM),
        scratch_shapes=[
            pltpu.VMEM((3, toks, channels), BF16),
            pltpu.VMEM((3, TAIL, channels), BF16),
            pltpu.VMEM(short_filter.shape, F32),
            pltpu.VMEM((modes, channels), F32),
            pltpu.VMEM((modes, channels), F32),
            pltpu.VMEM((2 * rows, toks), BF16),
            pltpu.VMEM((half, half), BF16),
            pltpu.VMEM((3, 2, tiles, rows, LANES), F32),
            pltpu.VMEM((2, tiles, half, LANES), F32),
            pltpu.VMEM((tiles, half, LANES), F32),
            pltpu.VMEM((tiles, half, LANES), F32),
            pltpu.VMEM((half, channels), BF16),
            pltpu.VMEM((half, channels), BF16),
            pltpu.VMEM((half, channels), BF16),
            pltpu.VMEM((channels, dout), BF16),
            pltpu.VMEM((half, WIDTH), F32),
            pltpu.VMEM((2, tiles, modes, CHUNKS, LANES), F32),
            pltpu.VMEM((tiles, modes, CHUNKS, LANES), F32),
            pltpu.VMEM((tiles, modes, CHUNKS, LANES), F32),
            pltpu.VMEM((tiles, step, CHUNKS, LANES), F32),
            pltpu.VMEM((8, channels), F32),
            pltpu.VMEM((8, channels), F32),
            pltpu.VMEM((modes, channels), BF16),
            pltpu.VMEM((modes, channels), BF16),
            pltpu.VMEM((modes, channels), BF16),
            pltpu.VMEM((n_ctx // 2, modes, channels), BF16),
            pltpu.VMEM((modes, channels), F32),
            pltpu.VMEM((modes, channels), F32),
            pltpu.VMEM((modes, channels), F32),
            pltpu.VMEM((modes, channels), F32),
            pltpu.VMEM((n_out, share, WIDTH), F32),
            pltpu.VMEM((n_out, share, WIDTH), F32),
            pltpu.VMEM((n_out, share, WIDTH), BF16),
            pltpu.VMEM((n_out, share, WIDTH), BF16),
            pltpu.VMEM((n_out, share, WIDTH), BF16),
            pltpu.VMEM((n_out, share, WIDTH), BF16),
            pltpu.VMEM((n_out, share, WIDTH), BF16),
            pltpu.VMEM((n_out, share, WIDTH), BF16),
            dma((GROUPS,)), dma((5,)), dma, dma((2,)),
            dma((GROUPS,)), dma((GROUPS,)),
            dma((n_ctx // 2, GROUPS)), dma((n_ctx // 2, GROUPS)),
            dma((n_out,)), dma((n_out,)), dma((n_out,)), dma((n_out,)),
            dma((n_out,)), dma((n_out,)),
        ],
        compiler_params=pltpu.CompilerParams(
            collective_id=0, has_side_effects=True, vmem_limit_bytes=48 * 2**20
        ),
    )(*operands)


def solution(mesh):
    placed = (
        P("ctx", None, "tp"),
        P(None, None, "tp"),
        P(None, "tp"),
        P(None, "tp"),
        P("tp", None),
    )
    return jax.shard_map(
        functools.partial(per_device, mesh.shape["ctx"]),
        mesh=mesh, in_specs=placed, out_specs=P(("ctx", "tp"), None), check_vma=False,
    )
```

time: 41.4 us -> 39.1 us (0.944)
  the two profiles are of different devices: /device:TPU:0 before, /device:TPU:25 now
where the time goes in v1:
time: 39.1 us; the launch traced here: 39 us
  Pallas kernels  38.2 us (98%)
  local copies, waits for them, and re-layouts  0.8 us (2%)
    pallas_call x1, Pallas kernels, per_device(): pl.pallas_call(functools.partial(kernel, n_ctx), out_shape=jax.ShapeDtype...  38.2 us
    unnamed x1, local copies, waits for them, and re-layouts  0.8 us

profile of v1, /device:TPU:25, one launch (start us, length us, event | category | flops | bytes accessed | tf_op | source)
XLA Modules:
  0.0 39.0 jit_solution(16910664287669475295)
XLA Ops:
  0.0 38.2 %shard_map.55 = bf16[64,4096]{1,0:T(8,128)(2,1)S(1)} custom-call(bf16[3,256,2048]{2,1,0:T(8,128)(2,1)} %bitcast.1, f32[3,3,2048]{2,1,0:T(4,128)} %taps_hbm.1, f32[16,2048]{1,0:T(8,128)} %rates_hbm.1, f32[16,2048]{1,0:T(8,128)} %res_hbm.1, bf16[2048,4096]{1,0:T(8,128)(2,1)} %w_hbm.1), custom_call_target="tpu_custom_call" | custom-call | tf_op jit(solution)/shard_map/pallas_call | solution.py:461
  38.2 0.8 %copy.7 = bf16[64,4096]{1,0:T(8,128)(2,1)} copy(bf16[64,4096]{1,0:T(8,128)(2,1)S(1)} %shard_map.55) | data formatting | bytes 1048576

commit v2 on v1

--- a/solution.py
+++ b/solution.py
@@ -9,7 +9,7 @@
 
 LANES = 128
 CHUNKS = 8
-GROUPS = 4
+UNITS = 4
 HALO_GROUP = 2
 MXU = 256
 WIDTH = 512
@@ -28,7 +28,7 @@
 
 def kernel(
     n_ctx, x_hbm, taps_hbm, rates_hbm, res_hbm, w_hbm, out_ref,
-    xb, tails, taps_ref, rates_ref, res_ref, order, back, xs, pf, qf, yl, gp, ga, gb, wv, pt, raw, base, fades, hb,
+    xb, tails, taps_ref, rates_ref, res_ref, order, back, xs_even, xs_odd, pf, qf, yl, gp, ga, gb, wv, pt, raw, base, fades, hb,
     halo_out, halo_in, st_out, twin_in, both_out, st_in,
     own_end, decay_all, carry, first, keep, kept, pair_out, pair_in, own_out, own_in, far_out, far_in,
     x_sem, in_sem, w_sem, halo_sem, twin_send, twin_recv, st_send, st_recv,
@@ -46,28 +46,23 @@
     half = toks // 2
     step = half // CHUNKS
     rows = half + 2 * CHUNKS
-    tiles = channels // LANES
-    per_group = tiles // GROUPS
-    gwidth = channels // GROUPS
-    blocks = gwidth // MXU
+    gwidth = UNITS * LANES
+    groups = channels // gwidth
     per_block = MXU // LANES
     n_out = w_hbm.shape[1] // WIDTH
     share = toks // 4
     early = 1 - chip
 
     def group(g):
-        return pl.ds(g * gwidth, gwidth)
+        return pl.ds(pl.multiple_of(g * gwidth, gwidth), gwidth)
 
     def x_copy(g):
-        return pltpu.make_async_copy(
-            x_hbm.at[1:3, :, group(g)], xb.at[1:3, :, group(g)], x_sem.at[g]
-        )
+        return pltpu.make_async_copy(x_hbm.at[:, :, group(g)], xb.at[:, :, group(g)], x_sem.at[g])
 
     tail_copy = pltpu.make_async_copy(x_hbm.at[:, toks - TAIL :, :], tails, in_sem.at[0])
     rates_copy = pltpu.make_async_copy(rates_hbm, rates_ref, in_sem.at[1])
     taps_copy = pltpu.make_async_copy(taps_hbm, taps_ref, in_sem.at[2])
     res_copy = pltpu.make_async_copy(res_hbm, res_ref, in_sem.at[3])
-    gate_copy = pltpu.make_async_copy(x_hbm.at[0], xb.at[0], in_sem.at[4])
     w_copy = pltpu.make_async_copy(w_hbm, wv, w_sem)
 
     rates_copy.start()
@@ -75,9 +70,11 @@
     x_copy(0).start()
     res_copy.start()
     tail_copy.start()
-    for g in range(1, GROUPS):
+
+    @pl.loop(1, groups)
+    def _(g):
         x_copy(g).start()
-    gate_copy.start()
+
     w_copy.start()
 
     barrier = pltpu.get_barrier_semaphore()
@@ -112,48 +109,84 @@
     def lanes(c):
         return pl.ds(pl.multiple_of(c * LANES, LANES), LANES)
 
-    def reorder(j, k):
-        cols = pl.ds(pl.multiple_of(k * MXU, MXU), MXU)
-        moved = jnp.dot(order[...], xb[j, :, cols], preferred_element_type=F32)
-        for b in range(2):
-            for t in range(per_block):
-                xs[j, b, k * per_block + t] = moved[b * rows : (b + 1) * rows, t * LANES : (t + 1) * LANES]
-
-    def feature(j, b, c, low, high):
-        lane = lanes(c)
+    def collapse(terms):
+        spot = place[0]
+        out = []
+        for f in range(0, len(terms), CHUNKS):
+            v = terms[f : f + CHUNKS]
+            low = spot < 4
+            y = [
+                jnp.where(low, v[n], v[n + 4]) + pltpu.roll(jnp.where(low, v[n + 4], v[n]), 4, 0)
+                for n in range(4)
+            ]
+            low = spot % 4 < 2
+            z = [
+                jnp.where(low, y[n] + pltpu.roll(y[n], 6, 0), y[n + 2] + pltpu.roll(y[n + 2], 2, 0))
+                for n in range(2)
+            ]
+            low = spot % 2 == 0
+            out.append(jnp.where(low, z[0] + pltpu.roll(z[0], 7, 0), z[1] + pltpu.roll(z[1], 1, 0)))
+        return jnp.concatenate(out, axis=0)
+
+    def over_chunks(terms):
+        return collapse([terms[n] for n in range(modes)])
+
+    def ordered(g, u):
+        return (xs_even, xs_odd)[u // per_block], g * per_block + u % per_block
+
+    def reorder(g, which):
+        cols = pl.ds(pl.multiple_of(g * gwidth + which * MXU, MXU), MXU)
+        for j in range(3):
+            moved = jnp.dot(order[...], xb[j, :, cols], preferred_element_type=F32)
+            for b in range(2):
+                for u in range(which * per_block, (which + 1) * per_block):
+                    xs, at = ordered(g, u)
+                    left = u % per_block * LANES
+                    xs[j, b, at] = moved[b * rows : (b + 1) * rows, left : left + LANES]
+
+    def feature(j, b, g, u, low, high):
+        lane = lanes(g * UNITS + u)
+        xs, where = ordered(g, u)
         total = None
         for i in range(3):
             at = (2 - i) * CHUNKS
-            term = taps_ref[i, j : j + 1, lane] * xs[j, b, c, at + low : at + high, :]
+            term = taps_ref[i, j : j + 1, lane] * xs[j, b, where, at + low : at + high, :]
             total = term if total is None else total + term
         return total
 
-    def ends(c):
+    def add_halo(j, g, u):
+        lane = lanes(g * UNITS + u)
+        xs, where = ordered(g, u)
+        xs[j, early, where, 0:1, :] = halo_in[2 * j : 2 * j + 1, lane]
+        xs[j, early, where, CHUNKS : CHUNKS + 1, :] = halo_in[2 * j + 1 : 2 * j + 2, lane]
+
+    def ends(g, u):
+        c = g * UNITS + u
         decay = spread(jnp.exp(-rates_ref[:, lanes(c)]))
         for b in range(2):
-            product = feature(1, b, c, 0, half) * feature(2, b, c, 0, half)
+            product = feature(1, b, g, u, 0, half) * feature(2, b, g, u, 0, half)
             pf[b, c] = product
             state = jnp.broadcast_to(product[None, :CHUNKS], (modes, CHUNKS, LANES))
             for i in range(1, step):
                 state = decay * state + product[None, i * CHUNKS : (i + 1) * CHUNKS]
             raw[b, c] = state
 
-    def finish(c):
+    def finish(g, u):
+        c = g * UNITS + u
         lane = lanes(c)
         rates = rates_ref[:, lane]
         decay = spread(jnp.exp(-rates))
         two = 2 * CHUNKS
         for j in (1, 2):
-            xs[j, early, c, 0:1, :] = halo_in[2 * j : 2 * j + 1, lane]
-            xs[j, early, c, CHUNKS : CHUNKS + 1, :] = halo_in[2 * j + 1 : 2 * j + 2, lane]
-        product = feature(1, early, c, 0, two) * feature(2, early, c, 0, two)
+            add_halo(j, g, u)
+        product = feature(1, early, g, u, 0, two) * feature(2, early, g, u, 0, two)
         change = product - pf[early, c, :two, :]
         pf[early, c, :two, :] = product
         grown = decay * change[None, :CHUNKS] + change[None, CHUNKS:]
-        raw[early, c] = raw[early, c] + spread(jnp.exp(-rates * float(step - 2))) * grown
-        whole = jnp.exp(-rates * float(half))
-        mixed = spread(whole) * raw[early, c] + raw[chip, c]
-        end = jnp.sum(jnp.exp(-spread(rates) * to_end) * mixed, axis=1)
+        fixed = raw[early, c] + spread(jnp.exp(-rates * float(step - 2))) * grown
+        raw[early, c] = fixed
+        mixed = spread(jnp.exp(-rates * float(half))) * fixed + raw[chip, c]
+        end = over_chunks(jnp.exp(-spread(rates) * to_end) * mixed)
         own_end[:, lane] = end
         st_out[:, lane] = end.astype(BF16)
         decay_all[:, lane] = jnp.exp(-rates * float(toks))
@@ -170,7 +203,7 @@
             total = None
             for k in range(i + 1):
                 at = (i - k) * CHUNKS
-                term = hb[c, k] * pf[b, c, at : at + CHUNKS, :]
+                term = hb[c, k : k + 1, :] * pf[b, c, at : at + CHUNKS, :]
                 total = term if total is None else total + term
             yl[c, i * CHUNKS : (i + 1) * CHUNKS, :] = total
 
@@ -179,31 +212,32 @@
         rates = rates_ref[:, lane]
         decay = jnp.exp(-rates)
         now = res_ref[:, lane] * jnp.sqrt(2.0 * rates)
+        terms = []
         for i in range(step):
-            hb[c, i] = jnp.broadcast_to(jnp.sum(now, axis=0, keepdims=True), (CHUNKS, LANES))
+            terms.append(summed(now.reshape(modes // CHUNKS, CHUNKS, LANES)))
             now = now * decay
-
-    def gates(b, c):
-        lane = lanes(c)
+        hb[c] = collapse(terms)
+
+    def gates(b, g, u):
         if b == 0:
-            xs[0, early, c, 0:1, :] = halo_in[0:1, lane]
-            xs[0, early, c, CHUNKS : CHUNKS + 1, :] = halo_in[1:2, lane]
-        qf[c] = feature(0, b, c, 0, half)
+            add_halo(0, g, u)
+        qf[g * UNITS + u] = feature(0, b, g, u, 0, half)
 
     def weights(lane, rates):
         return res_ref[:, lane] * jnp.sqrt(2.0 * rates) * jnp.exp(-rates)
 
-    def ahead(c):
+    def ahead(g, u):
+        c = g * UNITS + u
         lane = lanes(c)
         rates = rates_ref[:, lane]
         before, total = scanned(raw[0, c], rates)
-        other = jnp.sum(jnp.exp(-spread(rates) * to_end) * raw[1, c], axis=1)
+        other = over_chunks(jnp.exp(-spread(rates) * to_end) * raw[1, c])
         first[:, lane] = jnp.where(chip == 0, other, total)
         weight = spread(weights(lane, rates))
         into = jnp.exp(-spread(rates) * spots)
         fades[c] = weight * into * spread(jnp.exp(-rates * (float(half) * late_block)))
         base[c] = weight * (before + into * spread(other * late_block))
-        gates(0, c)
+        gates(0, g, u)
         near(0, c)
 
     def emit(c, state):
@@ -220,19 +254,20 @@
     def carried_tile(c):
         emit(c, base[c] + fades[c] * spread(carry[:, lanes(c)]))
 
-    def own_tile(c):
+    def own_tile(g, u):
+        c = g * UNITS + u
         lane = lanes(c)
         rates = rates_ref[:, lane]
         before, _ = scanned(raw[1, c], rates)
         into = carry[:, lane]
         into = jnp.where(chip == 1, jnp.exp(-rates * float(half)) * into + first[:, lane], into)
         state = spread(weights(lane, rates)) * (before + jnp.exp(-spread(rates) * spots) * spread(into))
-        gates(1, c)
+        gates(1, g, u)
         near(1, c)
         emit(c, state)
 
-    def restore(into, k):
-        cols = pl.ds(pl.multiple_of(k * MXU, MXU), MXU)
+    def restore(into, g):
+        cols = group(g)
         into[:, cols] = jnp.dot(back[...], gp[:, cols], preferred_element_type=F32).astype(BF16)
 
     halo_copy = pltpu.make_async_remote_copy(
@@ -267,42 +302,38 @@
         def _(dst):
             state_copy(g, pair, dst).start()
 
-    def group_ends(g):
-        x_copy(g).wait()
-
-        @pl.loop(g * blocks, (g + 1) * blocks)
-        def _(k):
-            for j in (1, 2):
-                reorder(j, k)
-
-            @pl.loop(k * per_block, (k + 1) * per_block)
-            def _(c):
-                ends(c)
-
-    def group_finish(g):
-        @pl.loop(g * per_group, (g + 1) * per_group)
-        def _(c):
-            finish(c)
-
-        twin_copy(g).start()
-
     tail_copy.wait()
     for j in range(3):
         halo_out[2 * j : 2 * j + 2, :] = tails[j].astype(F32)[TAIL - 2 :]
     halo_out[6:8, :] = jnp.zeros((2, channels), F32)
     rates_copy.wait()
     taps_copy.wait()
-    group_ends(0)
-
-    pl.semaphore_wait(barrier, n_ctx + 1)
-
-    @pl.when(me < n_ctx - 1)
-    def _():
-        halo_copy.start()
-
-    for g in range(1, GROUPS):
-        group_ends(g)
-        if g == HALO_GROUP:
+    x_copy(0).wait()
+    reorder(0, 0)
+
+    @pl.loop(0, groups)
+    def _(g):
+        @pl.when(g < groups - 1)
+        def _():
+            x_copy(g + 1).wait()
+
+        reorder(g, 1)
+        ends(g, 0)
+        ends(g, 1)
+        reorder((g + 1) % groups, 0)
+        ends(g, 2)
+        ends(g, 3)
+
+        @pl.when(g == 0)
+        def _():
+            pl.semaphore_wait(barrier, n_ctx + 1)
+
+            @pl.when(me < n_ctx - 1)
+            def _():
+                halo_copy.start()
+
+        @pl.when(g == HALO_GROUP)
+        def _():
             @pl.when(me == 0)
             def _():
                 halo_in[...] = jnp.zeros_like(halo_in)
@@ -311,30 +342,31 @@
             def _():
                 halo_copy.wait_recv()
 
-            for before in range(g):
-                group_finish(before)
-        if g >= HALO_GROUP:
-            group_finish(g)
+        low = jnp.where(g == HALO_GROUP, 0, g)
+        high = jnp.where(g < HALO_GROUP, low, g + 1)
+
+        @pl.loop(low, high)
+        def _(k):
+            for u in range(UNITS):
+                finish(k, u)
+            twin_copy(k).start()
 
     res_copy.wait()
-    gate_copy.wait()
-
-    for g in range(GROUPS):
-        @pl.loop(g * blocks, (g + 1) * blocks)
-        def _(k):
-            reorder(0, k)
-
-            @pl.loop(k * per_block, (k + 1) * per_block)
-            def _(c):
-                responses(c)
-                ahead(c)
-
-        if g == GROUPS - 2:
-            for sent in range(g + 1):
-                send_both(sent)
-    send_both(GROUPS - 1)
-
-    for g in range(GROUPS):
+
+    @pl.loop(0, groups)
+    def _(g):
+        for u in range(UNITS):
+            responses(g * UNITS + u)
+            ahead(g, u)
+
+        @pl.when(g == groups - 2)
+        def _():
+            @pl.loop(0, groups)
+            def _(k):
+                send_both(k)
+
+    @pl.loop(0, groups)
+    def _(g):
         cols = group(g)
         carry[:, cols] = jnp.zeros((modes, gwidth), F32)
 
@@ -348,13 +380,9 @@
         def _():
             carry[:, cols] = decay_all[:, cols] * carry[:, cols] + twin_in[:, cols].astype(F32)
 
-        @pl.loop(g * blocks, (g + 1) * blocks)
-        def _(k):
-            @pl.loop(k * per_block, (k + 1) * per_block)
-            def _(c):
-                carried_tile(c)
-
-            restore(ga, k)
+        for u in range(UNITS):
+            carried_tile(g * UNITS + u)
+        restore(ga, g)
 
     w_copy.wait()
 
@@ -401,13 +429,11 @@
 
     forward(n_out - 1)
 
-    @pl.loop(0, channels // MXU)
-    def _(k):
-        @pl.loop(k * per_block, (k + 1) * per_block)
-        def _(c):
-            own_tile(c)
-
-        restore(gb, k)
+    @pl.loop(0, groups)
+    def _(g):
+        for u in range(UNITS):
+            own_tile(g, u)
+        restore(gb, g)
 
     @pl.loop(0, n_out)
     def _(n):
@@ -429,7 +455,8 @@
         own_copy(n).wait_send()
         far_copy(n).wait_send()
 
-    for g in range(GROUPS):
+    @pl.loop(0, groups)
+    def _(g):
         twin_copy(g).wait_send()
 
         @pl.loop(pair + 1, n_ctx // 2)
@@ -447,6 +474,7 @@
     modes = decay_rates.shape[0]
     dout = out_weight.shape[1]
     tiles = channels // LANES
+    groups = tiles // UNITS
     n_out = dout // WIDTH
     share = toks // 4
     half = toks // 2
@@ -471,7 +499,8 @@
             pltpu.VMEM((modes, channels), F32),
             pltpu.VMEM((2 * rows, toks), BF16),
             pltpu.VMEM((half, half), BF16),
-            pltpu.VMEM((3, 2, tiles, rows, LANES), F32),
+            pltpu.VMEM((3, 2, tiles // 2, rows, LANES), F32),
+            pltpu.VMEM((3, 2, tiles // 2, rows, LANES), F32),
             pltpu.VMEM((2, tiles, half, LANES), F32),
             pltpu.VMEM((tiles, half, LANES), F32),
             pltpu.VMEM((tiles, half, LANES), F32),
@@ -483,7 +512,7 @@
             pltpu.VMEM((2, tiles, modes, CHUNKS, LANES), F32),
             pltpu.VMEM((tiles, modes, CHUNKS, LANES), F32),
             pltpu.VMEM((tiles, modes, CHUNKS, LANES), F32),
-            pltpu.VMEM((tiles, step, CHUNKS, LANES), F32),
+            pltpu.VMEM((tiles, step, LANES), F32),
             pltpu.VMEM((8, channels), F32),
             pltpu.VMEM((8, channels), F32),
             pltpu.VMEM((modes, channels), BF16),
@@ -502,9 +531,9 @@
             pltpu.VMEM((n_out, share, WIDTH), BF16),
             pltpu.VMEM((n_out, share, WIDTH), BF16),
             pltpu.VMEM((n_out, share, WIDTH), BF16),
-            dma((GROUPS,)), dma((5,)), dma, dma((2,)),
-            dma((GROUPS,)), dma((GROUPS,)),
-            dma((n_ctx // 2, GROUPS)), dma((n_ctx // 2, GROUPS)),
+            dma((groups,)), dma((4,)), dma, dma((2,)),
+            dma((groups,)), dma((groups,)),
+            dma((n_ctx // 2, groups)), dma((n_ctx // 2, groups)),
             dma((n_out,)), dma((n_out,)), dma((n_out,)), dma((n_out,)),
             dma((n_out,)), dma((n_out,)),
         ],

time: 39.1 us -> 36 us (0.921)
  Pallas kernels: 38.2 us -> 35.1 us
    pallas_call x1, Pallas kernels: 38.2 us -> 35.1 us  [per_device(): pl.pallas_call(functools.partial(kernel, n_ctx), out_shape=jax.ShapeDtype...]
where the time goes in v2:
time: 36 us; the launch traced here: 35.9 us
  Pallas kernels  35.1 us (98%)
  local copies, waits for them, and re-layouts  0.8 us (2%)
    pallas_call x1, Pallas kernels, per_device(): pl.pallas_call(functools.partial(kernel, n_ctx), out_shape=jax.ShapeDtype...  35.1 us
    unnamed x1, local copies, waits for them, and re-layouts  0.8 us

profile of v2, /device:TPU:25, one launch (start us, length us, event | category | flops | bytes accessed | tf_op | source)
XLA Modules:
  0.0 35.9 jit_solution(7637624024541458920)
XLA Ops:
  0.0 35.1 %shard_map.55 = bf16[64,4096]{1,0:T(8,128)(2,1)S(1)} custom-call(bf16[3,256,2048]{2,1,0:T(8,128)(2,1)} %bitcast.1, f32[3,3,2048]{2,1,0:T(4,128)} %taps_hbm.1, f32[16,2048]{1,0:T(8,128)} %rates_hbm.1, f32[16,2048]{1,0:T(8,128)} %res_hbm.1, bf16[2048,4096]{1,0:T(8,128)(2,1)} %w_hbm.1), custom_call_target="tpu_custom_call" | custom-call | tf_op jit(solution)/shard_map/pallas_call | solution.py:489
  35.1 0.8 %copy.7 = bf16[64,4096]{1,0:T(8,128)(2,1)} copy(bf16[64,4096]{1,0:T(8,128)(2,1)S(1)} %shard_map.55) | data formatting | bytes 1048576

commit v3 on v2

--- a/solution.py
+++ b/solution.py
@@ -13,6 +13,9 @@
 HALO_GROUP = 2
 MXU = 256
 WIDTH = 512
+FIRST = (1, 0)
+SECOND = (2, 1)
+LAG = 2
 TAIL = 16
 MESH = pl.DeviceIdType.MESH
 F32 = jnp.float32
@@ -47,6 +50,7 @@
     step = half // CHUNKS
     rows = half + 2 * CHUNKS
     gwidth = UNITS * LANES
+    tiles = channels // LANES
     groups = channels // gwidth
     per_block = MXU // LANES
     n_out = w_hbm.shape[1] // WIDTH
@@ -66,9 +70,9 @@
     w_copy = pltpu.make_async_copy(w_hbm, wv, w_sem)
 
     rates_copy.start()
+    res_copy.start()
+    x_copy(0).start()
     taps_copy.start()
-    x_copy(0).start()
-    res_copy.start()
     tail_copy.start()
 
     @pl.loop(1, groups)
@@ -160,36 +164,49 @@
         xs[j, early, where, 0:1, :] = halo_in[2 * j : 2 * j + 1, lane]
         xs[j, early, where, CHUNKS : CHUNKS + 1, :] = halo_in[2 * j + 1 : 2 * j + 2, lane]
 
-    def ends(g, u):
+    def ends(g, u, last=None):
         c = g * UNITS + u
-        decay = spread(jnp.exp(-rates_ref[:, lanes(c)]))
+        lane = lanes(c)
+        rates = spread(rates_ref[:, lane])
+        decay = jnp.exp(-rates)
+        mixed = None
         for b in range(2):
             product = feature(1, b, g, u, 0, half) * feature(2, b, g, u, 0, half)
             pf[b, c] = product
-            state = jnp.broadcast_to(product[None, :CHUNKS], (modes, CHUNKS, LANES))
+            opening = product[:CHUNKS]
+            if last is not None:
+                opening = opening + 0.0 * last
+            state = jnp.broadcast_to(opening[None], (modes, CHUNKS, LANES))
             for i in range(1, step):
                 state = decay * state + product[None, i * CHUNKS : (i + 1) * CHUNKS]
-            raw[b, c] = state
+            raw[b, c] = state.reshape(modes * CHUNKS, LANES)
+            last = state[modes - 1]
+            after = to_end + float(half) * (1.0 - late_block if b == 0 else late_block)
+            part = jnp.exp(-rates * after) * state
+            mixed = part if mixed is None else mixed + part
+        own_end[:, lane] = over_chunks(mixed)
+        return last
 
     def finish(g, u):
         c = g * UNITS + u
         lane = lanes(c)
         rates = rates_ref[:, lane]
-        decay = spread(jnp.exp(-rates))
         two = 2 * CHUNKS
         for j in (1, 2):
             add_halo(j, g, u)
         product = feature(1, early, g, u, 0, two) * feature(2, early, g, u, 0, two)
         change = product - pf[early, c, :two, :]
         pf[early, c, :two, :] = product
-        grown = decay * change[None, :CHUNKS] + change[None, CHUNKS:]
-        fixed = raw[early, c] + spread(jnp.exp(-rates * float(step - 2))) * grown
-        raw[early, c] = fixed
-        mixed = spread(jnp.exp(-rates * float(half))) * fixed + raw[chip, c]
-        end = over_chunks(jnp.exp(-spread(rates) * to_end) * mixed)
+        grown = jnp.exp(-rates) * change[:1] + change[CHUNKS : CHUNKS + 1]
+        grown = jnp.exp(-rates * float(step - 2)) * grown
+        heads = pl.ds(0, modes, stride=CHUNKS)
+        raw[early, c, heads, :] = raw[early, c, heads, :] + grown
+        end = own_end[:, lane] + jnp.exp(-rates * float(toks - step)) * grown
         own_end[:, lane] = end
         st_out[:, lane] = end.astype(BF16)
-        decay_all[:, lane] = jnp.exp(-rates * float(toks))
+
+    def states_of(b, c):
+        return raw[b, c].reshape(modes, CHUNKS, LANES)
 
     def scanned(state, rates):
         for reach in (1, 2, 4):
@@ -217,6 +234,7 @@
             terms.append(summed(now.reshape(modes // CHUNKS, CHUNKS, LANES)))
             now = now * decay
         hb[c] = collapse(terms)
+        decay_all[:, lane] = jnp.exp(-rates * float(toks))
 
     def gates(b, g, u):
         if b == 0:
@@ -230,8 +248,8 @@
         c = g * UNITS + u
         lane = lanes(c)
         rates = rates_ref[:, lane]
-        before, total = scanned(raw[0, c], rates)
-        other = over_chunks(jnp.exp(-spread(rates) * to_end) * raw[1, c])
+        before, total = scanned(states_of(0, c), rates)
+        other = over_chunks(jnp.exp(-spread(rates) * to_end) * states_of(1, c))
         first[:, lane] = jnp.where(chip == 0, other, total)
         weight = spread(weights(lane, rates))
         into = jnp.exp(-spread(rates) * spots)
@@ -258,7 +276,7 @@
         c = g * UNITS + u
         lane = lanes(c)
         rates = rates_ref[:, lane]
-        before, _ = scanned(raw[1, c], rates)
+        before, _ = scanned(states_of(1, c), rates)
         into = carry[:, lane]
         into = jnp.where(chip == 1, jnp.exp(-rates * float(half)) * into + first[:, lane], into)
         state = spread(weights(lane, rates)) * (before + jnp.exp(-spread(rates) * spots) * spread(into))
@@ -302,14 +320,29 @@
         def _(dst):
             state_copy(g, pair, dst).start()
 
+    rates_copy.wait()
+    res_copy.wait()
+
+    @pl.loop(0, tiles // 2)
+    def _(k):
+        responses(2 * k)
+        responses(2 * k + 1)
+
+    first_sent = jnp.where(odd == 1, FIRST[1], FIRST[0])
+    second = jnp.where(odd == 1, SECOND[1], SECOND[0])
     tail_copy.wait()
     for j in range(3):
         halo_out[2 * j : 2 * j + 2, :] = tails[j].astype(F32)[TAIL - 2 :]
     halo_out[6:8, :] = jnp.zeros((2, channels), F32)
-    rates_copy.wait()
     taps_copy.wait()
     x_copy(0).wait()
     reorder(0, 0)
+
+    pl.semaphore_wait(barrier, n_ctx + 1)
+
+    @pl.when(me < n_ctx - 1)
+    def _():
+        halo_copy.start()
 
     @pl.loop(0, groups)
     def _(g):
@@ -318,19 +351,9 @@
             x_copy(g + 1).wait()
 
         reorder(g, 1)
-        ends(g, 0)
-        ends(g, 1)
+        last = ends(g, 1, ends(g, 0))
         reorder((g + 1) % groups, 0)
-        ends(g, 2)
-        ends(g, 3)
-
-        @pl.when(g == 0)
-        def _():
-            pl.semaphore_wait(barrier, n_ctx + 1)
-
-            @pl.when(me < n_ctx - 1)
-            def _():
-                halo_copy.start()
+        ends(g, 3, ends(g, 2, last))
 
         @pl.when(g == HALO_GROUP)
         def _():
@@ -351,19 +374,18 @@
                 finish(k, u)
             twin_copy(k).start()
 
-    res_copy.wait()
-
     @pl.loop(0, groups)
     def _(g):
         for u in range(UNITS):
-            responses(g * UNITS + u)
             ahead(g, u)
 
-        @pl.when(g == groups - 2)
-        def _():
-            @pl.loop(0, groups)
-            def _(k):
-                send_both(k)
+        low = jnp.where(g == second, groups - 1, 0)
+        high = jnp.where(g == second, groups, jnp.where(g == first_sent, groups - 1, 0))
+
+        @pl.loop(low, high)
+        def _(k):
+            send_both(k)
+
 
     @pl.loop(0, groups)
     def _(g):
@@ -423,11 +445,13 @@
         pair_copy(n).start()
         keep[n] = pt[mine, :]
 
-        @pl.when(n > 0)
+        @pl.when(n >= LAG)
         def _():
-            forward(n - 1)
-
-    forward(n_out - 1)
+            forward(n - LAG)
+
+    @pl.loop(n_out - LAG, n_out)
+    def _(n):
+        forward(n)
 
     @pl.loop(0, groups)
     def _(g):
@@ -509,7 +533,7 @@
             pltpu.VMEM((half, channels), BF16),
             pltpu.VMEM((channels, dout), BF16),
             pltpu.VMEM((half, WIDTH), F32),
-            pltpu.VMEM((2, tiles, modes, CHUNKS, LANES), F32),
+            pltpu.VMEM((2, tiles, modes * CHUNKS, LANES), F32),
             pltpu.VMEM((tiles, modes, CHUNKS, LANES), F32),
             pltpu.VMEM((tiles, modes, CHUNKS, LANES), F32),
             pltpu.VMEM((tiles, step, LANES), F32),

time: 36 us -> 34 us (0.944)
  the two profiles are of different devices: /device:TPU:25 before, /device:TPU:0 now
where the time goes in v3:
time: 34 us; the launch traced here: 33.4 us
  Pallas kernels  32.6 us (96%)
  local copies, waits for them, and re-layouts  0.8 us (2%)
    pallas_call x1, Pallas kernels, per_device(): pl.pallas_call(functools.partial(kernel, n_ctx), out_shape=jax.ShapeDtype...  32.6 us
    unnamed x1, local copies, waits for them, and re-layouts  0.8 us

profile of v3, /device:TPU:0, one launch (start us, length us, event | category | flops | bytes accessed | tf_op | source)
XLA Modules:
  0.0 33.4 jit_solution(17891399887705451829)
XLA Ops:
  0.0 32.6 %shard_map.55 = bf16[64,4096]{1,0:T(8,128)(2,1)S(1)} custom-call(bf16[3,256,2048]{2,1,0:T(8,128)(2,1)} %bitcast.1, f32[3,3,2048]{2,1,0:T(4,128)} %taps_hbm.1, f32[16,2048]{1,0:T(8,128)} %rates_hbm.1, f32[16,2048]{1,0:T(8,128)} %res_hbm.1, bf16[2048,4096]{1,0:T(8,128)(2,1)} %w_hbm.1), custom_call_target="tpu_custom_call" | custom-call | tf_op jit(solution)/shard_map/pallas_call | solution.py:513
  32.7 0.8 %copy.7 = bf16[64,4096]{1,0:T(8,128)(2,1)} copy(bf16[64,4096]{1,0:T(8,128)(2,1)S(1)} %shard_map.55) | data formatting | bytes 1048576

commit v4 on v3

--- a/solution.py
+++ b/solution.py
@@ -31,7 +31,7 @@
 
 def kernel(
     n_ctx, x_hbm, taps_hbm, rates_hbm, res_hbm, w_hbm, out_ref,
-    xb, tails, taps_ref, rates_ref, res_ref, order, back, xs_even, xs_odd, pf, qf, yl, gp, ga, gb, wv, pt, raw, base, fades, hb,
+    xb, tails, taps_ref, rates_ref, res_ref, order, back, xs_even, xs_odd, pf, qf, yl, gp, ga, gb, wv, pt, raw, base, fades, entry, hb,
     halo_out, halo_in, st_out, twin_in, both_out, st_in,
     own_end, decay_all, carry, first, keep, kept, pair_out, pair_in, own_out, own_in, far_out, far_in,
     x_sem, in_sem, w_sem, halo_sem, twin_send, twin_recv, st_send, st_recv,
@@ -103,8 +103,6 @@
     back[...] = jnp.where(token == (row % CHUNKS) * step + row // CHUNKS, 1.0, 0.0).astype(BF16)
 
     place = lax.broadcasted_iota(jnp.int32, (1, CHUNKS, LANES), 1)
-    spots = place.astype(F32) * float(step)
-    to_end = float((CHUNKS - 1) * step) - spots
     late_block = jnp.where(chip == 0, 1.0, 0.0).astype(F32)
 
     def spread(values):
@@ -132,9 +130,6 @@
             out.append(jnp.where(low, z[0] + pltpu.roll(z[0], 7, 0), z[1] + pltpu.roll(z[1], 1, 0)))
         return jnp.concatenate(out, axis=0)
 
-    def over_chunks(terms):
-        return collapse([terms[n] for n in range(modes)])
-
     def ordered(g, u):
         return (xs_even, xs_odd)[u // per_block], g * per_block + u % per_block
 
@@ -164,12 +159,12 @@
         xs[j, early, where, 0:1, :] = halo_in[2 * j : 2 * j + 1, lane]
         xs[j, early, where, CHUNKS : CHUNKS + 1, :] = halo_in[2 * j + 1 : 2 * j + 2, lane]
 
+    def chunk(b, c, s):
+        return raw[b, c, s * (modes + 1) : s * (modes + 1) + modes, :]
+
     def ends(g, u, last=None):
         c = g * UNITS + u
-        lane = lanes(c)
-        rates = spread(rates_ref[:, lane])
-        decay = jnp.exp(-rates)
-        mixed = None
+        decay = jnp.exp(-spread(rates_ref[:, lanes(c)]))
         for b in range(2):
             product = feature(1, b, g, u, 0, half) * feature(2, b, g, u, 0, half)
             pf[b, c] = product
@@ -179,12 +174,9 @@
             state = jnp.broadcast_to(opening[None], (modes, CHUNKS, LANES))
             for i in range(1, step):
                 state = decay * state + product[None, i * CHUNKS : (i + 1) * CHUNKS]
-            raw[b, c] = state.reshape(modes * CHUNKS, LANES)
+            for n in range(modes):
+                raw[b, c, pl.ds(n, CHUNKS, stride=modes + 1), :] = state[n]
             last = state[modes - 1]
-            after = to_end + float(half) * (1.0 - late_block if b == 0 else late_block)
-            part = jnp.exp(-rates * after) * state
-            mixed = part if mixed is None else mixed + part
-        own_end[:, lane] = over_chunks(mixed)
         return last
 
     def finish(g, u):
@@ -198,22 +190,16 @@
         change = product - pf[early, c, :two, :]
         pf[early, c, :two, :] = product
         grown = jnp.exp(-rates) * change[:1] + change[CHUNKS : CHUNKS + 1]
-        grown = jnp.exp(-rates * float(step - 2)) * grown
-        heads = pl.ds(0, modes, stride=CHUNKS)
-        raw[early, c, heads, :] = raw[early, c, heads, :] + grown
-        end = own_end[:, lane] + jnp.exp(-rates * float(toks - step)) * grown
+        end = chunk(early, c, 0) + jnp.exp(-rates * float(step - 2)) * grown
+        raw[early, c, 0:modes, :] = end
+        fade = jnp.exp(-rates * float(step))
+        for s in range(1, CHUNKS):
+            end = fade * end + chunk(early, c, s)
+        first[:, lane] = end
+        for s in range(CHUNKS):
+            end = fade * end + chunk(chip, c, s)
         own_end[:, lane] = end
         st_out[:, lane] = end.astype(BF16)
-
-    def states_of(b, c):
-        return raw[b, c].reshape(modes, CHUNKS, LANES)
-
-    def scanned(state, rates):
-        for reach in (1, 2, 4):
-            fade = spread(jnp.exp(-rates * float(step * reach)))
-            moved = pltpu.roll(state, reach, 1)
-            state = state + jnp.where(place >= reach, fade * moved, 0.0)
-        return jnp.where(place >= 1, pltpu.roll(state, 1, 1), 0.0), state[:, CHUNKS - 1, :]
 
     def near(b, c):
         for i in range(step):
@@ -248,41 +234,60 @@
         c = g * UNITS + u
         lane = lanes(c)
         rates = rates_ref[:, lane]
-        before, total = scanned(states_of(0, c), rates)
-        other = over_chunks(jnp.exp(-spread(rates) * to_end) * states_of(1, c))
-        first[:, lane] = jnp.where(chip == 0, other, total)
-        weight = spread(weights(lane, rates))
-        into = jnp.exp(-spread(rates) * spots)
-        fades[c] = weight * into * spread(jnp.exp(-rates * (float(half) * late_block)))
-        base[c] = weight * (before + into * spread(other * late_block))
+        weight = weights(lane, rates)
+        fade = jnp.exp(-rates * float(step))
+        state = first[:, lane] * late_block
+        reach = weight * jnp.exp(-rates * (float(half) * late_block))
+        for s in range(CHUNKS):
+            base[c, s] = weight * state
+            fades[c, s] = reach
+            if s < CHUNKS - 1:
+                state = fade * state + chunk(0, c, s)
+                reach = fade * reach
         gates(0, g, u)
         near(0, c)
 
-    def emit(c, state):
+    def enter(u, s, state):
+        entry[u, pl.ds(s, modes, stride=CHUNKS + 1), :] = state
+
+    def emit(c, u):
         lane = lanes(c)
         decay = spread(jnp.exp(-rates_ref[:, lane]))
+        state = [entry[u, n * (CHUNKS + 1) : n * (CHUNKS + 1) + CHUNKS, :] for n in range(modes)]
         for i in range(0, step, 2):
             parts = []
             for k in (i, i + 1):
                 at = slice(k * CHUNKS, (k + 1) * CHUNKS)
-                parts.append(qf[c, at, :] * (yl[c, at, :] + summed(state)))
-                state = decay * state
+                terms = state
+                while len(terms) > 1:
+                    middle = len(terms) // 2
+                    terms = [terms[n] + terms[n + middle] for n in range(middle)]
+                parts.append(qf[c, at, :] * (yl[c, at, :] + terms[0]))
+                state = [decay[n] * state[n] for n in range(modes)]
             gp[i * CHUNKS : (i + 2) * CHUNKS, lane] = jnp.concatenate(parts, axis=0).astype(BF16)
 
-    def carried_tile(c):
-        emit(c, base[c] + fades[c] * spread(carry[:, lanes(c)]))
+    def carried_tile(g, u):
+        c = g * UNITS + u
+        into = carry[:, lanes(c)]
+        for s in range(CHUNKS):
+            enter(u, s, base[c, s] + fades[c, s] * into)
+        emit(c, u)
 
     def own_tile(g, u):
         c = g * UNITS + u
         lane = lanes(c)
         rates = rates_ref[:, lane]
-        before, _ = scanned(states_of(1, c), rates)
-        into = carry[:, lane]
-        into = jnp.where(chip == 1, jnp.exp(-rates * float(half)) * into + first[:, lane], into)
-        state = spread(weights(lane, rates)) * (before + jnp.exp(-spread(rates) * spots) * spread(into))
+        weight = weights(lane, rates)
+        fade = jnp.exp(-rates * float(step))
+        state = carry[:, lane]
+        state = jnp.where(chip == 1, jnp.exp(-rates * float(half)) * state + first[:, lane], state)
+        for s in range(CHUNKS):
+            enter(u, s, weight * state)
+            if s < CHUNKS - 1:
+                state = fade * state + chunk(1, c, s)
         gates(1, g, u)
         near(1, c)
-        emit(c, state)
+        emit(c, u)
 
     def restore(into, g):
         cols = group(g)
@@ -403,7 +408,7 @@
             carry[:, cols] = decay_all[:, cols] * carry[:, cols] + twin_in[:, cols].astype(F32)
 
         for u in range(UNITS):
-            carried_tile(g * UNITS + u)
+            carried_tile(g, u)
         restore(ga, g)
 
     w_copy.wait()
@@ -533,9 +538,10 @@
             pltpu.VMEM((half, channels), BF16),
             pltpu.VMEM((channels, dout), BF16),
             pltpu.VMEM((half, WIDTH), F32),
-            pltpu.VMEM((2, tiles, modes * CHUNKS, LANES), F32),
-            pltpu.VMEM((tiles, modes, CHUNKS, LANES), F32),
-            pltpu.VMEM((tiles, modes, CHUNKS, LANES), F32),
+            pltpu.VMEM((2, tiles, CHUNKS * (modes + 1), LANES), F32),
+            pltpu.VMEM((tiles, CHUNKS, modes, LANES), F32),
+            pltpu.VMEM((tiles, CHUNKS, modes, LANES), F32),
+            pltpu.VMEM((UNITS, modes * (CHUNKS + 1), LANES), F32),
             pltpu.VMEM((tiles, step, LANES), F32),
             pltpu.VMEM((8, channels), F32),
             pltpu.VMEM((8, channels), F32),

time: 34 us -> 33.1 us (0.974); the launches traced: 33.4 us -> 33 us
  Pallas kernels: 32.6 us -> 32.1 us
    pallas_call x1, Pallas kernels: 32.6 us -> 32.1 us  [per_device(): pl.pallas_call(functools.partial(kernel, n_ctx), out_shape=jax.ShapeDtype...]
where the time goes in v4:
time: 33.1 us; the launch traced here: 33 us
  Pallas kernels  32.1 us (97%)
  local copies, waits for them, and re-layouts  0.8 us (2%)
    pallas_call x1, Pallas kernels, per_device(): pl.pallas_call(functools.partial(kernel, n_ctx), out_shape=jax.ShapeDtype...  32.1 us
    unnamed x1, local copies, waits for them, and re-layouts  0.8 us

profile of v4, /device:TPU:0, one launch (start us, length us, event | category | flops | bytes accessed | tf_op | source)
XLA Modules:
  0.0 33.0 jit_solution(3702591083524151043)
XLA Ops:
  0.0 32.1 %shard_map.55 = bf16[64,4096]{1,0:T(8,128)(2,1)S(1)} custom-call(bf16[3,256,2048]{2,1,0:T(8,128)(2,1)} %bitcast.1, f32[3,3,2048]{2,1,0:T(4,128)} %taps_hbm.1, f32[16,2048]{1,0:T(8,128)} %rates_hbm.1, f32[16,2048]{1,0:T(8,128)} %res_hbm.1, bf16[2048,4096]{1,0:T(8,128)(2,1)} %w_hbm.1), custom_call_target="tpu_custom_call" | custom-call | tf_op jit(solution)/shard_map/pallas_call | solution.py:518
  32.2 0.8 %copy.7 = bf16[64,4096]{1,0:T(8,128)(2,1)} copy(bf16[64,4096]{1,0:T(8,128)(2,1)S(1)} %shard_map.55) | data formatting | bytes 1048576

commit v5 on v4

--- a/solution.py
+++ b/solution.py
@@ -10,11 +10,11 @@
 LANES = 128
 CHUNKS = 8
 UNITS = 4
-HALO_GROUP = 2
+HALO_GROUP = 3
 MXU = 256
 WIDTH = 512
-FIRST = (1, 0)
-SECOND = (2, 1)
+FIRST = (2, 2)
+SECOND = (3, 3)
 LAG = 2
 TAIL = 16
 MESH = pl.DeviceIdType.MESH
@@ -343,12 +343,6 @@
     x_copy(0).wait()
     reorder(0, 0)
 
-    pl.semaphore_wait(barrier, n_ctx + 1)
-
-    @pl.when(me < n_ctx - 1)
-    def _():
-        halo_copy.start()
-
     @pl.loop(0, groups)
     def _(g):
         @pl.when(g < groups - 1)
@@ -359,6 +353,14 @@
         last = ends(g, 1, ends(g, 0))
         reorder((g + 1) % groups, 0)
         ends(g, 3, ends(g, 2, last))
+
+        @pl.when(g == 0)
+        def _():
+            pl.semaphore_wait(barrier, n_ctx + 1)
+
+            @pl.when(me < n_ctx - 1)
+            def _():
+                halo_copy.start()
 
         @pl.when(g == HALO_GROUP)
         def _():

time: 33.1 us -> 32.5 us (0.982)
  Pallas kernels: 32.1 us -> 31.3 us
    pallas_call x1, Pallas kernels: 32.1 us -> 31.3 us  [per_device(): pl.pallas_call(functools.partial(kernel, n_ctx), out_shape=jax.ShapeDtype...]
where the time goes in v5:
time: 32.5 us; the launch traced here: 32.1 us
  Pallas kernels  31.3 us (96%)
  local copies, waits for them, and re-layouts  0.8 us (2%)
    pallas_call x1, Pallas kernels, per_device(): pl.pallas_call(functools.partial(kernel, n_ctx), out_shape=jax.ShapeDtype...  31.3 us
    unnamed x1, local copies, waits for them, and re-layouts  0.8 us

profile of v5, /device:TPU:0, one launch (start us, length us, event | category | flops | bytes accessed | tf_op | source)
XLA Modules:
  0.0 32.1 jit_solution(6295957644065514276)
XLA Ops:
  0.0 31.3 %shard_map.55 = bf16[64,4096]{1,0:T(8,128)(2,1)S(1)} custom-call(bf16[3,256,2048]{2,1,0:T(8,128)(2,1)} %bitcast.1, f32[3,3,2048]{2,1,0:T(4,128)} %taps_hbm.1, f32[16,2048]{1,0:T(8,128)} %rates_hbm.1, f32[16,2048]{1,0:T(8,128)} %res_hbm.1, bf16[2048,4096]{1,0:T(8,128)(2,1)} %w_hbm.1), custom_call_target="tpu_custom_call" | custom-call | tf_op jit(solution)/shard_map/pallas_call | solution.py:520
  31.3 0.8 %copy.7 = bf16[64,4096]{1,0:T(8,128)(2,1)} copy(bf16[64,4096]{1,0:T(8,128)(2,1)S(1)} %shard_map.55) | data formatting | bytes 1048576

commit v6 on v5

--- a/solution.py
+++ b/solution.py
@@ -475,6 +475,23 @@
 
     @pl.loop(0, n_out)
     def _(n):
+        pair_copy(n).wait_send()
+        own_copy(n).wait_send()
+
+    @pl.loop(0, groups)
+    def _(g):
+        twin_copy(g).wait_send()
+
+        @pl.loop(pair + 1, n_ctx // 2)
+        def _(dst):
+            state_copy(g, pair, dst).wait_send()
+
+    @pl.when(me < n_ctx - 1)
+    def _():
+        halo_copy.wait_send()
+
+    @pl.loop(0, n_out)
+    def _(n):
         own_copy(n).wait_recv()
         far_copy(n).wait_recv()
         total = kept[n] + own_in[n].astype(F32) + far_in[n].astype(F32)
@@ -482,21 +499,7 @@
 
     @pl.loop(0, n_out)
     def _(n):
-        pair_copy(n).wait_send()
-        own_copy(n).wait_send()
         far_copy(n).wait_send()
-
-    @pl.loop(0, groups)
-    def _(g):
-        twin_copy(g).wait_send()
-
-        @pl.loop(pair + 1, n_ctx // 2)
-        def _(dst):
-            state_copy(g, pair, dst).wait_send()
-
-    @pl.when(me < n_ctx - 1)
-    def _():
-        halo_copy.wait_send()
 
 
 def per_device(n_ctx, projections, short_filter, decay_rates, residues, out_weight):

time: 32.5 us -> 32.4 us (level)
  no operation moved by 1% of the time
where the time goes in v6:
time: 32.4 us; the launch traced here: 32 us
  Pallas kernels  31.2 us (96%)
  local copies, waits for them, and re-layouts  0.8 us (2%)
    pallas_call x1, Pallas kernels, per_device(): pl.pallas_call(functools.partial(kernel, n_ctx), out_shape=jax.ShapeDtype...  31.2 us
    unnamed x1, local copies, waits for them, and re-layouts  0.8 us

profile of v6, /device:TPU:0, one launch (start us, length us, event | category | flops | bytes accessed | tf_op | source)
XLA Modules:
  0.0 32.0 jit_solution(361802447335167173)
XLA Ops:
  0.0 31.2 %shard_map.55 = bf16[64,4096]{1,0:T(8,128)(2,1)S(1)} custom-call(bf16[3,256,2048]{2,1,0:T(8,128)(2,1)} %bitcast.1, f32[3,3,2048]{2,1,0:T(4,128)} %taps_hbm.1, f32[16,2048]{1,0:T(8,128)} %rates_hbm.1, f32[16,2048]{1,0:T(8,128)} %res_hbm.1, bf16[2048,4096]{1,0:T(8,128)(2,1)} %w_hbm.1), custom_call_target="tpu_custom_call" | custom-call | tf_op jit(solution)/shard_map/pallas_call | solution.py:523
  31.2 0.8 %copy.7 = bf16[64,4096]{1,0:T(8,128)(2,1)} copy(bf16[64,4096]{1,0:T(8,128)(2,1)S(1)} %shard_map.55) | data formatting | bytes 1048576
